TPU v7x, 32 devices: a whole 2x2x4 slice. The times are simulated.
32 devices in a mesh: row: 16 (over z, x, core), col: 2 (over y).
Axes of the slice: x: 2, y: 2, z: 4, core: 2. Of those that a mesh axis runs over, the one named last changes fastest.
Arguments:
- coefficients: float32 [2, 1, 256, 256, 256], P(None, None, 'col', 'row'), may hold values from -6 to 6
- real_bands: float32 [2, 256, 256, 256], P(None, 'col', 'row'), may hold values from -6 to 6
Outputs:
- spline_coefs: float32 [2, 1, 256, 256, 256], P(None, None, None, ('row', 'col'))
- spline_table: float32 [2, 256, 256, 256], P('col', 'row')
All inputs are finite; a program needn't handle non-finite values.
Results may differ from a plain program's by a relative error of at most 0.00007.
Values sent between devices are 32-bit elements; how exact they have to be, the bound alone decides.
A program may use at most 64 MiB of HBM per device.

v0:
```python
import math

import jax
import jax.numpy as jnp
from jax import lax
from jax.sharding import PartitionSpec as P

highest = lax.Precision.HIGHEST


def dft_tables(length):
    counter = jnp.arange(length, dtype=jnp.int32)
    phase = (counter[:, None] * counter[None, :] % length).astype(jnp.float32)
    angle = phase * (2.0 * math.pi / length)
    spread = counter.astype(jnp.float32) * (2.0 * math.pi / length)
    weight = 6.0 / ((4.0 + 2.0 * jnp.cos(spread)) * math.sqrt(length))
    return (jnp.cos(angle) * weight[:, None], jnp.sin(angle) * weight[:, None])


def reshaped(tables, shape):
    return tuple((table.reshape(shape) for table in tables))


def apply_complex(stacked, tables, form):
    cosine, sine_table = tables

    def single(left, right):
        return jnp.einsum(form, left, right, precision=highest)

    real_part = single(stacked[0], cosine) - single(stacked[1], sine_table)
    imag_part = single(stacked[0], sine_table) + single(stacked[1], cosine)
    return jnp.stack([real_part, imag_part])


def local(coefficients, real_bands):
    rows = lax.axis_size("row")
    cols = lax.axis_size("col")
    band_count = coefficients.shape[1]
    z_local = coefficients.shape[2]
    y_local = coefficients.shape[3]
    x_length = coefficients.shape[4]
    z_full = z_local * cols
    y_full = y_local * rows
    x_tables = dft_tables(x_length)
    y_tables = dft_tables(y_full)
    z_tables = dft_tables(z_full)
    turned = jnp.transpose(real_bands, (0, 3, 2, 1))
    by_band = lax.all_to_all(turned, "col", split_axis=0, concat_axis=3, tiled=True)
    spline_table = lax.all_to_all(by_band, "row", split_axis=1, concat_axis=2, tiled=True)
    x_rows = x_length // rows
    x_final = x_rows // cols
    first = apply_complex(
        coefficients, reshaped(x_tables, (x_length, rows, cols, x_final)), "bzyk,kjcq->bzcjqy"
    )
    first = first.reshape(2, band_count, z_local, cols, rows * x_final * y_local)
    z_view = reshaped(z_tables, (cols, z_local, z_full))
    moved = lax.all_to_all(first, "col", split_axis=3, concat_axis=4, tiled=True)
    items = moved.shape[1]
    moved = moved.reshape(2, items, z_local, cols, rows, x_final, y_local)
    second = apply_complex(moved, z_view, "bzsjqy,szn->bjnqy")
    second = second.reshape(2, band_count, rows, z_full, x_final * y_local)
    y_view = reshaped(y_tables, (rows, y_local, y_full))
    moved = lax.all_to_all(second, "row", split_axis=2, concat_axis=4, tiled=True)
    items = moved.shape[1]
    moved = moved.reshape(2, items, z_full, rows, x_final, y_local)
    spline_coefs = apply_complex(moved, y_view, "bnsqy,syk->bnqk")
    return (spline_coefs, spline_table)


def solution(mesh):
    placed = (P(None, None, "col", "row", None), P(None, "col", "row", None))
    return jax.shard_map(
        local,
        mesh=mesh,
        in_specs=placed,
        out_specs=(P(None, None, None, ("row", "col"), None), P("col", "row", None, None)),
        check_vma=False,
    )
```

profile of v0, /device:TPU:11, one launch (start us, length us, event | category | flops | bytes accessed | tf_op | source)
XLA Modules:
  0.0 342.2 jit_solution(14566584639126745965)
XLA Ops:
  0.7 2.7 fusion.114
  3.4 3.9 %fusion.3 = f32[16,2,8,128,16]{3,2,4,1,0:T(8,128)S(1)} fusion(f32[1,1,128,16,256]{4,3,2,1,0:T(8,128)S(1)} %get-tuple-element.15, f32[256]{0:T(256)S(1)} %multiply_divide_fusion.1, s32[16,2,8]{2,1,0:T(2,128)S(1)} %multiply_add_fusion), kind=kOutput, calls=%fused_computation.15 | convolution fusion | flops 1611595776 | bytes 4196352 | tf_op jit(solution)/shard_map/bzyk,kjcq->bzcjqy/dot_general | solution.py:28
  7.2 3.9 %fusion.2 = f32[16,2,8,128,16]{3,2,4,1,0:T(8,128)S(1)} fusion(f32[1,1,128,16,256]{4,3,2,1,0:T(8,128)S(1)} %get-tuple-element.15, f32[256]{0:T(256)S(1)} %multiply_divide_fusion.1, s32[16,2,8]{2,1,0:T(2,128)S(1)} %multiply_add_fusion), kind=kOutput, calls=%fused_computation.14 | convolution fusion | flops 1611595776 | bytes 4196352 | tf_op jit(solution)/shard_map/bzyk,kjcq->bzcjqy/dot_general | solution.py:28
  11.1 16.7 %subtract_bitcast_fusion = f32[1,128,2,16,8,16]{1,4,5,2,3,0:T(8,128)S(1)} fusion(f32[16,2,8,128,16]{3,2,4,1,0:T(8,128)S(1)} %fusion.3, f32[1,1,128,16,256]{4,3,2,1,0:T(8,128)S(1)} %get-tuple-element.14, f32[256]{0:T(256)S(1)} %multiply_divide_fusion.1, s32[16,2,8]{2,1,0:T(2,128)S(1)} %multiply_add_fusion), kind=kOutput, calls=%fused_computation.13 | convolution fusion | flops 1612120064 | bytes 6293504 | tf_op jit(solution)/shard_map/bzyk,kjcq->bzcjqy/dot_general | solution.py:28
  27.8 0.4 copy.38
  28.2 3.9 %add_bitcast_fusion = f32[1,128,2,16,8,16]{1,4,5,2,3,0:T(8,128)S(1)} fusion(f32[16,2,8,128,16]{3,2,4,1,0:T(8,128)S(1)} %fusion.2, f32[1,1,128,16,256]{4,3,2,1,0:T(8,128)S(1)} %get-tuple-element.14, f32[256]{0:T(256)S(1)} %multiply_divide_fusion.1, s32[16,2,8]{2,1,0:T(2,128)S(1)} %multiply_add_fusion), kind=kOutput, calls=%fused_computation.12 | convolution fusion | flops 1612120064 | bytes 6293504 | tf_op jit(solution)/shard_map/bzyk,kjcq->bzcjqy/dot_general | solution.py:28
  32.1 0.4 copy.39
  32.8 2.3 copy.40
  35.1 5.6 %all-to-all-start = ((f32[2,1,128,2,2048]{2,4,1,0,3:T(8,128)}), f32[2,1,128,2,2048]{2,4,1,0,3:T(8,128)}, u32[]{:S(2)}, u32[]{:S(2)}) async-start(f32[2,1,128,2,2048]{2,4,1,0,3:T(8,128)} %copy.40), calls=%async_computation | async-start | bytes 8388608 | tf_op jit(solution)/shard_map/all_to_all | solution.py:57
  40.7 46.7 %all-to-all-done = f32[2,1,128,2,2048]{2,4,1,0,3:T(8,128)} async-done(((f32[2,1,128,2,2048]{2,4,1,0,3:T(8,128)}), f32[2,1,128,2,2048]{2,4,1,0,3:T(8,128)}, u32[]{:S(2)}, u32[]{:S(2)}) %all-to-all-start) | async-done | bytes 4194336 | tf_op jit(solution)/shard_map/all_to_all | solution.py:57
  87.5 5.6 %all-to-all-start.2 = ((f32[2,256,16,128]{1,2,3,0:T(8,128)}), f32[2,256,16,128]{1,2,3,0:T(8,128)}, u32[]{:S(2)}, u32[]{:S(2)}) async-start(f32[2,256,16,128]{1,2,3,0:T(8,128)} %bitcast.170), calls=%async_computation.2 | async-start | bytes 8388608 | tf_op jit(solution)/shard_map/all_to_all | solution.py:48
  93.1 2.5 fusion.113
  95.6 2.9 fusion.19
  98.6 2.9 fusion.15
  101.5 3.0 bitcast_subtract_fusion
  104.5 3.4 bitcast_add_fusion
  107.9 2.4 pad_maximum_fusion.1
  110.3 28.7 %all-to-all-done.2 = f32[2,256,16,128]{1,2,3,0:T(8,128)} async-done(((f32[2,256,16,128]{1,2,3,0:T(8,128)}), f32[2,256,16,128]{1,2,3,0:T(8,128)}, u32[]{:S(2)}, u32[]{:S(2)}) %all-to-all-start.2) | async-done | bytes 4194336 | tf_op jit(solution)/shard_map/all_to_all | solution.py:48
  138.9 8.3 %all-to-all-start.1 = ((f32[2,1,16,256,128]{3,4,0,1,2:T(8,128)}), f32[2,1,16,256,128]{3,4,0,1,2:T(8,128)}, u32[]{:S(2)}, u32[]{:S(2)}) async-start(f32[2,1,16,256,128]{3,4,0,1,2:T(8,128)} %pad_maximum_fusion.1), calls=%async_computation.1 | async-start | bytes 8388608 | tf_op jit(solution)/shard_map/all_to_all | solution.py:63
  147.3 5.6 %copy.65 = f32[1,256,16,256]{3,2,0,1:T(8,128)} copy(f32[1,256,16,256]{1,2,3,0:T(8,128)} %bitcast.74) | data formatting | bytes 8388608 | tf_op jit(solution)/shard_map/all_to_all | solution.py:48
  152.8 86.9 %all-to-all-done.1 = f32[2,1,16,256,128]{3,4,0,1,2:T(8,128)} async-done(((f32[2,1,16,256,128]{3,4,0,1,2:T(8,128)}), f32[2,1,16,256,128]{3,4,0,1,2:T(8,128)}, u32[]{:S(2)}, u32[]{:S(2)}) %all-to-all-start.1) | async-done | bytes 4194336 | tf_op jit(solution)/shard_map/all_to_all | solution.py:63
  239.8 4.9 %all-to-all-start.3 = ((f32[1,256,16,256]{3,2,0,1:T(8,128)}), f32[1,256,16,256]{3,2,0,1:T(8,128)}, u32[]{:S(2)}, u32[]{:S(2)}) async-start(f32[1,256,16,256]{3,2,0,1:T(8,128)} %copy.65), calls=%async_computation.3 | async-start | bytes 8388608 | tf_op jit(solution)/shard_map/all_to_all | solution.py:49
  244.7 2.5 copy.81
  247.3 0.4 fusion.112
  247.7 4.4 %fusion.22 = f32[256,8,256,1]{2,0,1,3:T(8,128)S(1)} fusion(f32[256,16,8,16]{0,3,2,1:T(8,128)S(1)} %bitcast.180, f32[16,16]{1,0:T(8,128)S(1)} %multiply_divide_fusion, s32[16,16]{1,0:T(8,128)S(1)} %multiply_add_fusion.1), kind=kOutput, calls=%fused_computation.43 | convolution fusion | flops 1611595776 | bytes 4196352 | tf_op jit(solution)/shard_map/bnsqy,syk->bnqk/dot_general | solution.py:28
  252.1 4.5 %fusion.24 = f32[256,8,256,1]{2,0,1,3:T(8,128)S(1)} fusion(f32[256,16,8,16]{0,3,2,1:T(8,128)S(1)} %bitcast.181, f32[16,16]{1,0:T(8,128)S(1)} %multiply_divide_fusion, s32[16,16]{1,0:T(8,128)S(1)} %multiply_add_fusion.1), kind=kOutput, calls=%fused_computation.45 | convolution fusion | flops 1611595776 | bytes 4196352 | tf_op jit(solution)/shard_map/bnsqy,syk->bnqk/dot_general | solution.py:28
  256.6 4.5 %fusion.1 = f32[1,1,256,8,256]{4,2,3,1,0:T(8,128)S(1)} fusion(f32[256,8,256,1]{2,0,1,3:T(8,128)S(1)} %fusion.22, f32[256,16,8,16]{0,3,2,1:T(8,128)S(1)} %bitcast.174, f32[16,16]{1,0:T(8,128)S(1)} %multiply_divide_fusion, s32[16,16]{1,0:T(8,128)S(1)} %multiply_add_fusion.1), kind=kOutput, calls=%fused_computation.11 | convolution fusion | flops 1612120064 | bytes 6293504 | tf_op jit(solution)/shard_map/bnsqy,syk->bnqk/dot_general | solution.py:28
  261.2 4.4 %fusion = f32[1,1,256,8,256]{4,2,3,1,0:T(8,128)S(1)} fusion(f32[256,8,256,1]{2,0,1,3:T(8,128)S(1)} %fusion.24, f32[256,16,8,16]{0,3,2,1:T(8,128)S(1)} %bitcast.175, f32[16,16]{1,0:T(8,128)S(1)} %multiply_divide_fusion, s32[16,16]{1,0:T(8,128)S(1)} %multiply_add_fusion.1), kind=kOutput, calls=%fused_computation.9 | convolution fusion | flops 1612120064 | bytes 6293504 | tf_op jit(solution)/shard_map/bnsqy,syk->bnqk/dot_general | solution.py:28
  265.6 0.4 pad_maximum_fusion.2
  266.0 4.4 %copy.52 = f32[2,1,256,8,256]{4,3,2,1,0:T(8,128)} copy(f32[2,1,256,8,256]{4,2,3,1,0:T(8,128)S(1)} %pad_maximum_fusion.2) | data formatting | bytes 8388608
  270.4 66.7 %all-to-all-done.3 = f32[1,256,16,256]{3,2,0,1:T(8,128)} async-done(((f32[1,256,16,256]{3,2,0,1:T(8,128)}), f32[1,256,16,256]{3,2,0,1:T(8,128)}, u32[]{:S(2)}, u32[]{:S(2)}) %all-to-all-start.3) | async-done | bytes 4194336 | tf_op jit(solution)/shard_map/all_to_all | solution.py:49
  337.1 4.8 %copy.51 = f32[1,16,16,16,256]{4,3,2,1,0:T(8,128)} copy(f32[1,16,16,16,256]{4,3,1,2,0:T(8,128)} %bitcast.76) | data formatting | bytes 8388608 | tf_op jit(solution)/shard_map/all_to_all | solution.py:49
  (7 shorter events, 0.5 us)
Async XLA Ops:
  35.1 52.4 %all-to-all-start = ((f32[2,1,128,2,2048]{2,4,1,0,3:T(8,128)}), f32[2,1,128,2,2048]{2,4,1,0,3:T(8,128)}, u32[]{:S(2)}, u32[]{:S(2)}) async-start(f32[2,1,128,2,2048]{2,4,1,0,3:T(8,128)} %copy.40), calls=%async_computation | async-start | bytes 8388608 | tf_op jit(solution)/shard_map/all_to_all | solution.py:57
  87.5 51.5 %all-to-all-start.2 = ((f32[2,256,16,128]{1,2,3,0:T(8,128)}), f32[2,256,16,128]{1,2,3,0:T(8,128)}, u32[]{:S(2)}, u32[]{:S(2)}) async-start(f32[2,256,16,128]{1,2,3,0:T(8,128)} %bitcast.170), calls=%async_computation.2 | async-start | bytes 8388608 | tf_op jit(solution)/shard_map/all_to_all | solution.py:48
  138.9 100.8 %all-to-all-start.1 = ((f32[2,1,16,256,128]{3,4,0,1,2:T(8,128)}), f32[2,1,16,256,128]{3,4,0,1,2:T(8,128)}, u32[]{:S(2)}, u32[]{:S(2)}) async-start(f32[2,1,16,256,128]{3,4,0,1,2:T(8,128)} %pad_maximum_fusion.1), calls=%async_computation.1 | async-start | bytes 8388608 | tf_op jit(solution)/shard_map/all_to_all | solution.py:63
  239.8 97.4 %all-to-all-start.3 = ((f32[1,256,16,256]{3,2,0,1:T(8,128)}), f32[1,256,16,256]{3,2,0,1:T(8,128)}, u32[]{:S(2)}, u32[]{:S(2)}) async-start(f32[1,256,16,256]{3,2,0,1:T(8,128)} %copy.65), calls=%async_computation.3 | async-start | bytes 8388608 | tf_op jit(solution)/shard_map/all_to_all | solution.py:49
where the time goes:
time: 345 us; the launch traced here: 342 us
  waiting for transfers between devices  229 us (66%)
  matrix products  58.4 us (17%)
  local copies, waits for them, and re-layouts  26.1 us (8%)
  starting transfers between devices  24.4 us (7%)
    all_to_all x1, waiting for transfers between devices, local(): lax.all_to_all(second, 'row', split_axis=2, concat_axis=4, tiled=True)  86.9 us
    all_to_all x1, waiting for transfers between devices, local(): lax.all_to_all(by_band, 'row', split_axis=1, concat_axis=2, tiled=True)  66.7 us
    dot_general x12, matrix products, single(): return jnp.einsum(form, left, right, precision=highest)  58.4 us
    all_to_all x1, waiting for transfers between devices, local(): lax.all_to_all(first, 'col', split_axis=3, concat_axis=4, tiled=True)  46.7 us
    all_to_all x1, waiting for transfers between devices, local(): lax.all_to_all(turned, 'col', split_axis=0, concat_axis=3, tiled=True)  28.7 us
    all_to_all x1, starting transfers between devices, local(): lax.all_to_all(second, 'row', split_axis=2, concat_axis=4, tiled=True)  8.34 us
  transfers between devices with their start and end apart: 4, of which 4 were waited for; matrix products, arithmetic and copies ran while one was open for 14% of the time, Pallas kernels for 0%

commit v1 on v0

v1 whole, which is shorter than its diff:
```python
import math

import jax
import jax.numpy as jnp
import numpy as np
from jax import lax
from jax.sharding import PartitionSpec as P

precision = lax.Precision.HIGH
axes = ("row", "col")


def transform_table(length):
    counter = np.arange(length)
    angle = (counter[:, None] * counter[None, :] % length) * (2.0 * math.pi / length)
    weight = 6.0 / ((4.0 + 2.0 * np.cos(counter * (2.0 * math.pi / length))) * math.sqrt(length))
    cosine = np.cos(angle) * weight[:, None]
    sine = np.sin(angle) * weight[:, None]
    table = np.stack([np.stack([cosine, sine], 1), np.stack([-sine, cosine], 1)])
    return table.astype(np.float32)


def local(coefficients, real_bands):
    rows = lax.axis_size("row")
    cols = lax.axis_size("col")
    devices = rows * cols
    _, bands, z_local, y_local, x_full = coefficients.shape
    z_full = z_local * cols
    y_full = y_local * rows
    x_final = x_full // devices
    table_bands = real_bands.shape[0] // cols
    x_rows = x_full // rows

    turned = real_bands.reshape(cols, table_bands, z_local, y_local, rows, x_rows)
    turned = jnp.transpose(turned, (4, 0, 1, 5, 3, 2))
    turned = turned.reshape(devices, table_bands, x_rows, y_local, z_local)
    placed = lax.all_to_all(turned, axes, split_axis=0, concat_axis=0, tiled=True)
    placed = placed.reshape(rows, cols, table_bands, x_rows, y_local, z_local)
    spline_table = jnp.transpose(placed, (2, 3, 0, 4, 1, 5)).reshape(table_bands, x_rows, y_full, z_full)

    x_table = transform_table(x_full).reshape(2, x_full, 2, devices, x_final)
    z_table = transform_table(z_full).reshape(2, cols, z_local, 2, z_full)
    y_table = transform_table(y_full).reshape(2, rows, y_local, 2, y_full)
    first = jnp.einsum("cbzyk,ckedq->debyqz", coefficients, x_table, precision=precision)
    moved = lax.all_to_all(first, axes, split_axis=0, concat_axis=0, tiled=True)
    moved = moved.reshape(rows, cols, 2, bands, y_local, x_final, z_local)
    second = jnp.einsum("rjebyqz,ejzfn->fbnqry", moved, z_table, precision=precision)
    spline_coefs = jnp.einsum("fbnqry,fryhk->hbnqk", second, y_table, precision=precision)
    return spline_coefs, spline_table


def solution(mesh):
    placed = (P(None, None, "col", "row", None), P(None, "col", "row", None))
    return jax.shard_map(
        local,
        mesh=mesh,
        in_specs=placed,
        out_specs=(P(None, None, None, ("row", "col"), None), P("col", "row", None, None)),
        check_vma=False,
    )
```

time: 345 us -> 218 us (0.63)
  the two profiles are of different devices: /device:TPU:11 before, /device:TPU:1 now
where the time goes in v1:
time: 218 us; the launch traced here: 217 us
  waiting for transfers between devices  159 us (73%)
  local copies, waits for them, and re-layouts  27.5 us (13%)
  matrix products  18.3 us (8%)
  starting transfers between devices  11.3 us (5%)
    all_to_all x1, waiting for transfers between devices, local(): moved = lax.all_to_all(first, axes, split_axis=0, concat_axis=0, tiled=True)  81.9 us
    all_to_all x1, waiting for transfers between devices, local(): lax.all_to_all(turned, axes, split_axis=0, concat_axis=0, tiled=True)  77.4 us
    unnamed x7, local copies, waits for them, and re-layouts  13.2 us
    all_to_all x1, starting transfers between devices, local(): moved = lax.all_to_all(first, axes, split_axis=0, concat_axis=0, tiled=True)  7.16 us
    dot_general x1, matrix products, local(): jnp.einsum('cbzyk,ckedq->debyqz', coefficients, x_table, precision=precis...  7.07 us
    transpose x1, local copies, waits for them, and re-layouts, local(): turned = jnp.transpose(turned, (4, 0, 1, 5, 3, 2))  6.57 us
    dot_general x1, matrix products, local(): jnp.einsum('rjebyqz,ejzfn->fbnqry', moved, z_table, precision=precision)  5.94 us
    transpose x1, local copies, waits for them, and re-layouts, local(): jnp.transpose(placed, (2, 3, 0, 4, 1, 5))  5.42 us
  transfers between devices with their start and end apart: 2, of which 2 were waited for; matrix products, arithmetic and copies ran while one was open for 13% of the time, Pallas kernels for 0%

profile of v1, /device:TPU:1, one launch (start us, length us, event | category | flops | bytes accessed | tf_op | source)
XLA Modules:
  0.0 217.0 jit_solution(17809909195561039393)
XLA Ops:
  0.6 7.1 %fusion.11 = f32[32,2,1,16,8,128]{5,4,3,0,1,2:T(8,128)S(1)} fusion(f32[2,256,2,32,8,1]{1,4,0,5,3,2:T(8,128)} %constant.11, f32[2,128,16,256,1,1]{3,2,1,0,5,4:T(8,128)} %bitcast.63), kind=kOutput, calls=%fused_computation.9 | convolution fusion | flops 3221225472 | bytes 9437184 | tf_op jit(solution)/shard_map/cbzyk,ckedq->debyqz/dot_general | solution.py:44
  7.7 2.3 %copy.35 = f32[32,2,1,16,8,128]{5,4,3,1,2,0:T(8,128)} copy(f32[32,2,1,16,8,128]{5,4,3,0,1,2:T(8,128)S(1)} %fusion.11) | data formatting | bytes 8388608 | tf_op jit(solution)/shard_map/cbzyk,ckedq->debyqz/transpose | solution.py:44
  10.0 7.2 %all-to-all-start = ((f32[32,2,1,16,8,128]{5,4,3,1,2,0:T(8,128)}), f32[32,2,1,16,8,128]{5,4,3,1,2,0:T(8,128)}, u32[]{:S(2)}, u32[]{:S(2)}) async-start(f32[32,2,1,16,8,128]{5,4,3,1,2,0:T(8,128)} %copy.35), calls=%async_computation | async-start | bytes 8388608 | tf_op jit(solution)/shard_map/all_to_all | solution.py:45
  17.2 5.3 %copy.38 = f32[2,128,16,256]{1,3,2,0:T(8,128)} copy(f32[2,128,16,256]{3,2,1,0:T(8,128)} %param.6) | data formatting | bytes 8388608 | tf_op args[1]
  22.5 6.6 %copy.39 = f32[16,2,1,16,16,128]{5,4,3,1,0,2:T(8,128)} copy(f32[16,2,1,16,16,128]{5,3,0,4,1,2:T(8,128)} %bitcast.62) | data formatting | bytes 8388608 | tf_op jit(solution)/shard_map/transpose | solution.py:35
  29.0 81.9 %all-to-all-done = f32[32,2,1,16,8,128]{5,4,3,1,2,0:T(8,128)} async-done(((f32[32,2,1,16,8,128]{5,4,3,1,2,0:T(8,128)}), f32[32,2,1,16,8,128]{5,4,3,1,2,0:T(8,128)}, u32[]{:S(2)}, u32[]{:S(2)}) %all-to-all-start) | async-done | bytes 4194336 | tf_op jit(solution)/shard_map/all_to_all | solution.py:45
  110.9 0.0 copy-start.1
  110.9 4.2 %all-to-all-start.1 = ((f32[32,1,16,16,128]{4,3,2,1,0:T(8,128)}), f32[32,1,16,16,128]{4,3,2,1,0:T(8,128)}, u32[]{:S(2)}, u32[]{:S(2)}) async-start(f32[32,1,16,16,128]{4,3,2,1,0:T(8,128)} %bitcast.60), calls=%async_computation.1 | async-start | bytes 8388608 | tf_op jit(solution)/shard_map/all_to_all | solution.py:37
  115.1 0.0 copy-done.1
  115.1 0.0 copy-start
  115.1 5.9 %fusion.14 = f32[2,256,8,16,16]{1,4,2,3,0:T(8,128)S(1)} fusion(f32[2,2,128,2,256,1,1]{4,2,1,0,6,5,3:T(8,128)S(1)} %copy-done.1, f32[16,2,2,16,8,128]{5,4,3,2,1,0:T(8,128)} %bitcast.12), kind=kOutput, calls=%fused_computation.10 | convolution fusion | flops 3221225472 | bytes 9437184 | tf_op jit(solution)/shard_map/rjebyqz,ejzfn->fbnqry/dot_general | solution.py:47
  121.1 0.0 copy-done
  121.1 5.3 %fusion.8 = f32[2,1,256,8,256]{2,4,3,0,1:T(8,128)} fusion(f32[2,16,16,2,256,1]{4,2,1,0,5,3:T(8,128)S(1)} %copy-done, f32[2,256,8,16,16]{1,4,2,3,0:T(8,128)S(1)} %fusion.14), kind=kOutput, calls=%fused_computation.8 | convolution fusion | flops 3221225472 | bytes 9437184 | tf_op jit(solution)/shard_map/fbnqry,fryhk->hbnqk/dot_general | solution.py:48
  126.4 5.4 %copy.42 = f32[2,1,256,8,256]{4,3,2,1,0:T(8,128)} copy(f32[2,1,256,8,256]{2,4,3,0,1:T(8,128)} %fusion.8) | data formatting | bytes 8388608
  131.8 77.4 %all-to-all-done.1 = f32[32,1,16,16,128]{4,3,2,1,0:T(8,128)} async-done(((f32[32,1,16,16,128]{4,3,2,1,0:T(8,128)}), f32[32,1,16,16,128]{4,3,2,1,0:T(8,128)}, u32[]{:S(2)}, u32[]{:S(2)}) %all-to-all-start.1) | async-done | bytes 4194336 | tf_op jit(solution)/shard_map/all_to_all | solution.py:37
  209.2 5.4 %copy.41 = f32[1,16,16,16,2,128]{5,4,0,3,2,1:T(2,128)S(1)} copy(f32[1,16,16,16,2,128]{5,3,1,4,2,0:T(8,128)} %bitcast.29) | data formatting | bytes 8388608 | tf_op jit(solution)/shard_map/transpose | solution.py:39
  214.6 2.4 %copy.43 = f32[1,16,256,256]{3,2,1,0:T(8,128)} copy(f32[1,16,256,256]{3,0,2,1:T(1,128)S(1)} %bitcast.61) | data formatting | bytes 8388608
Async XLA Ops:
  10.0 101.0 %all-to-all-start = ((f32[32,2,1,16,8,128]{5,4,3,1,2,0:T(8,128)}), f32[32,2,1,16,8,128]{5,4,3,1,2,0:T(8,128)}, u32[]{:S(2)}, u32[]{:S(2)}) async-start(f32[32,2,1,16,8,128]{5,4,3,1,2,0:T(8,128)} %copy.35), calls=%async_computation | async-start | bytes 8388608 | tf_op jit(solution)/shard_map/all_to_all | solution.py:45
  110.9 4.2 %copy-start.1 = (f32[2,2,128,2,256,1,1]{4,2,1,0,6,5,3:T(8,128)S(1)}, f32[2,2,128,2,256,1,1]{4,2,1,0,6,5,3:T(8,128)}, u32[]{:S(2)}) copy-start(f32[2,2,128,2,256,1,1]{4,2,1,0,6,5,3:T(8,128)} %constant.10) | copy-start | bytes 3145732
  110.9 98.2 %all-to-all-start.1 = ((f32[32,1,16,16,128]{4,3,2,1,0:T(8,128)}), f32[32,1,16,16,128]{4,3,2,1,0:T(8,128)}, u32[]{:S(2)}, u32[]{:S(2)}) async-start(f32[32,1,16,16,128]{4,3,2,1,0:T(8,128)} %bitcast.60), calls=%async_computation.1 | async-start | bytes 8388608 | tf_op jit(solution)/shard_map/all_to_all | solution.py:37
  115.1 6.0 %copy-start = (f32[2,16,16,2,256,1]{4,2,1,0,5,3:T(8,128)S(1)}, f32[2,16,16,2,256,1]{4,2,1,0,5,3:T(8,128)}, u32[]{:S(2)}) copy-start(f32[2,16,16,2,256,1]{4,2,1,0,5,3:T(8,128)} %constant.9) | copy-start | bytes 3145732

commit v2 on v1

--- a/solution.py
+++ b/solution.py
@@ -1,13 +1,20 @@
+import functools
 import math
 
 import jax
 import jax.numpy as jnp
+import ml_dtypes
 import numpy as np
 from jax import lax
+from jax.experimental import pallas as pl
+from jax.experimental.pallas import tpu as pltpu
 from jax.sharding import PartitionSpec as P
 
 precision = lax.Precision.HIGH
 axes = ("row", "col")
+MESH = pl.DeviceIdType.MESH
+LANES = 128
+SUBLANES = 8
 
 
 def transform_table(length):
@@ -20,7 +27,301 @@
     return table.astype(np.float32)
 
 
+def split_table(table):
+    high = table.astype(ml_dtypes.bfloat16)
+    low = (table - high.astype(np.float32)).astype(ml_dtypes.bfloat16)
+    return np.stack([high, low])
+
+
+def split(values):
+    high = values.astype(jnp.bfloat16)
+    return high, (values - high.astype(jnp.float32)).astype(jnp.bfloat16)
+
+
+def product(left, right, contract):
+    def one(a, b):
+        return lax.dot_general(a, b, (contract, ((), ())), preferred_element_type=jnp.float32)
+
+    return one(left[0], right[0]) + (one(left[0], right[1]) + one(left[1], right[0]))
+
+
+def kernel(
+    rows, cols, y_local,
+    coefficients, bands, x_table, z_table, y_table,
+    out, table_out,
+    source, band_in, x_parts, z_parts, y_parts, turned, first, arrived, result,
+    load_sem, local_sem, first_send, first_recv, band_send, band_recv,
+):
+    row, col = lax.axis_index("row"), lax.axis_index("col")
+    half_rows = rows // 2
+    half, place = row // half_rows, row % half_rows
+    x_tiles, y_tiles = source.shape[1], result.shape[1]
+    x_full = x_tiles * LANES
+    x_rows = x_full // rows
+    y_full = y_local * rows
+    z_full = LANES * cols
+    block = y_local * SUBLANES
+
+    def target(by_col, by_half, step):
+        to_row = (half + by_half) % 2 * half_rows + (place + step) % half_rows
+        return to_row, (col + by_col) % cols
+
+    def origin(by_col, by_half, step):
+        from_row = (half + by_half) % 2 * half_rows + (place - step + half_rows) % half_rows
+        return from_row, (col - by_col + cols) % cols
+
+    def number(by_col, by_half, step):
+        return (by_col * 2 + by_half) * half_rows + step
+
+    groups = [(by_col, by_half) for by_half in (1, 0) for by_col in range(cols)]
+
+    def each_step(group, do):
+        own = group == (0, 0)
+
+        def body(step, _):
+            do(*group, step)
+            return 0
+
+        lax.fori_loop(1 if own else 0, half_rows, body, 0)
+
+    barrier = pltpu.get_barrier_semaphore()
+
+    def greet(by_col, by_half, step):
+        pl.semaphore_signal(barrier, inc=1, device_id=target(by_col, by_half, step), device_id_type=MESH)
+
+    for group in groups:
+        each_step(group, greet)
+
+    def load(k, src, dst):
+        return pltpu.make_async_copy(src, dst, load_sem.at[k])
+
+    def load_band(b, tile):
+        return load(b * x_tiles + tile, bands.at[b, :, pl.ds(tile * LANES, LANES)], band_in.at[b, tile])
+
+    k = cols * x_tiles
+    loads = [
+        load(k, x_table, x_parts),
+        load(k + 1, z_table, z_parts),
+        load(k + 2, y_table, y_parts),
+    ]
+    for tile in range(x_tiles):
+        loads.append(load(k + 3 + tile, coefficients.at[:, :, pl.ds(tile * LANES, LANES)], source.at[:, tile]))
+    for by_col in range(cols):
+        for tile in range(x_tiles):
+            load_band((col + by_col) % cols, tile).start()
+    for one in loads:
+        one.start()
+
+    def turn(by_col, by_half):
+        b = (col + by_col) % cols
+        half_tiles = x_tiles // 2
+        lead = (half + by_half) % 2 * half_tiles
+        flat = turned.reshape(cols, x_full * y_local, LANES)
+
+        def body(y, _):
+            for at in range(half_tiles):
+                plane = band_in[b, lead + at, pl.ds(y, LANES, stride=y_local), :]
+                flat[b, pl.ds((lead + at) * LANES * y_local + y, LANES, stride=y_local), :] = plane.T
+            return 0
+
+        lax.fori_loop(0, y_local, body, 0)
+
+    def band_copy(by_col, by_half, step, place_row, place_col):
+        k = number(by_col, by_half, step)
+        to_row, to_col = target(by_col, by_half, step)
+        return pltpu.make_async_remote_copy(
+            src_ref=turned.at[to_col, pl.ds(to_row * x_rows, x_rows)],
+            dst_ref=table_out.at[
+                :,
+                pl.ds(pl.multiple_of(place_row * y_local, SUBLANES), y_local),
+                pl.ds(pl.multiple_of(place_col * LANES, LANES), LANES),
+            ],
+            send_sem=band_send.at[k],
+            recv_sem=band_recv.at[k],
+            device_id=(to_row, to_col),
+            device_id_type=MESH,
+        )
+
+    def first_copy(by_col, by_half, step, place_row, place_col):
+        k = number(by_col, by_half, step)
+        to_row, to_col = target(by_col, by_half, step)
+        return pltpu.make_async_remote_copy(
+            src_ref=first.at[to_row * cols + to_col],
+            dst_ref=arrived.at[place_col, :, pl.ds(pl.multiple_of(place_row * block, SUBLANES), block)],
+            send_sem=first_send.at[k],
+            recv_sem=first_recv.at[k],
+            device_id=(to_row, to_col),
+            device_id_type=MESH,
+        )
+
+    def send_band(by_col, by_half, step):
+        band_copy(by_col, by_half, step, row, col).start()
+
+    for tile in range(x_tiles):
+        load_band(col, tile).wait()
+    turn(0, 1)
+    pl.semaphore_wait(barrier, rows * cols - 1)
+    each_step((0, 1), send_band)
+
+    for one in loads:
+        one.wait()
+
+    def x_step(pair, _):
+        y = pair * 2
+        parts = []
+        for part in range(2):
+            for tile in range(x_tiles):
+                lines = [source[part, tile, pl.ds(y + j, LANES, stride=y_local), :] for j in range(2)]
+                parts.append(jnp.concatenate(lines, axis=0))
+        lines = split(jnp.concatenate(parts, axis=1))
+        made = product((x_parts[0], x_parts[1]), lines, ((1,), (1,)))
+        for part in range(2):
+            for j in range(2):
+                piece = made[part * x_full : (part + 1) * x_full, j * LANES : (j + 1) * LANES]
+                at = pl.multiple_of((y + j) * SUBLANES, SUBLANES)
+                first[:, part, pl.ds(at, SUBLANES), :] = piece.reshape(rows * cols, SUBLANES, LANES)
+        return 0
+
+    lax.fori_loop(0, y_local // 2, x_step, 0)
+
+    def send_first(step, _):
+        for group in groups:
+            if group == (0, 0):
+
+                @pl.when(step > 0)
+                def _():
+                    first_copy(*group, step, row, col).start()
+
+            else:
+                first_copy(*group, step, row, col).start()
+        return 0
+
+    lax.fori_loop(0, half_rows, send_first, 0)
+    own_first = pltpu.make_async_copy(
+        first.at[row * cols + col],
+        arrived.at[col, :, pl.ds(pl.multiple_of(row * block, SUBLANES), block)],
+        local_sem.at[0],
+    )
+    own_first.start()
+
+    for by_col in range(1, cols):
+        for tile in range(x_tiles):
+            load_band((col + by_col) % cols, tile).wait()
+    for group in groups:
+        if group != (0, 1):
+            turn(*group)
+            each_step(group, send_band)
+    own_band = pltpu.make_async_copy(
+        turned.at[col, pl.ds(row * x_rows, x_rows)],
+        table_out.at[
+            :,
+            pl.ds(pl.multiple_of(row * y_local, SUBLANES), y_local),
+            pl.ds(pl.multiple_of(col * LANES, LANES), LANES),
+        ],
+        local_sem.at[1],
+    )
+    own_band.start()
+
+    own_first.wait()
+    for group in groups:
+        each_step(group, lambda *at: first_copy(*at, *origin(*at)).wait_recv())
+
+    def final_step(x, _):
+        pieces = [
+            arrived[c, part, pl.ds(x, y_full, stride=SUBLANES), :] for part in range(2) for c in range(cols)
+        ]
+        lines = split(jnp.concatenate(pieces, axis=1))
+        second = product((z_parts[0], z_parts[1]), lines, ((1,), (1,)))
+        lines = split(jnp.concatenate([second[:z_full], second[z_full:]], axis=1))
+        third = product(lines, (y_parts[0], y_parts[1]), ((1,), (0,)))
+        for part in range(2):
+            for tile in range(y_tiles):
+                at = part * y_full + tile * LANES
+                result[part, tile, pl.ds(x, z_full, stride=SUBLANES), :] = third[:, at : at + LANES]
+        return 0
+
+    lax.fori_loop(0, SUBLANES, final_step, 0)
+    stores = [
+        pltpu.make_async_copy(result.at[:, tile], out.at[:, :, pl.ds(tile * LANES, LANES)], local_sem.at[2 + tile])
+        for tile in range(y_tiles)
+    ]
+    for store in stores:
+        store.start()
+    for store in stores:
+        store.wait()
+    own_band.wait()
+    for group in groups:
+        each_step(group, lambda *at: first_copy(*at, *origin(*at)).wait_send())
+        each_step(group, lambda *at: band_copy(*at, *origin(*at)).wait_send())
+        each_step(group, lambda *at: band_copy(*at, *origin(*at)).wait_recv())
+
+
+def fused(coefficients, real_bands, rows, cols):
+    _, _, z_local, y_local, x_full = coefficients.shape
+    z_full, y_full, devices = z_local * cols, y_local * rows, rows * cols
+    x_rows = x_full // rows
+    x_table = split_table(np.transpose(transform_table(x_full), (2, 3, 0, 1)).reshape(2 * x_full, 2 * x_full))
+    z_table = split_table(np.transpose(transform_table(z_full), (2, 3, 0, 1)).reshape(2 * z_full, 2 * z_full))
+    y_table = split_table(transform_table(y_full).reshape(2 * y_full, 2 * y_full))
+    flops = 3 * 2 * 2 * 2 * (x_full + y_full + z_full) * coefficients.size
+    out, table = pl.pallas_call(
+        functools.partial(kernel, rows, cols, y_local),
+        out_shape=[
+            jax.ShapeDtypeStruct((2, z_full * SUBLANES, y_full), jnp.float32),
+            jax.ShapeDtypeStruct((x_rows, y_full, z_full), jnp.float32),
+        ],
+        in_specs=[pl.BlockSpec(memory_space=pl.ANY)] * 5,
+        out_specs=[pl.BlockSpec(memory_space=pl.ANY)] * 2,
+        scratch_shapes=[
+            pltpu.VMEM((2, x_full // LANES, z_local * y_local, LANES), jnp.float32),
+            pltpu.VMEM((cols, x_full // LANES, z_local * y_local, LANES), jnp.float32),
+            pltpu.VMEM(x_table.shape, jnp.bfloat16),
+            pltpu.VMEM(z_table.shape, jnp.bfloat16),
+            pltpu.VMEM(y_table.shape, jnp.bfloat16),
+            pltpu.VMEM((cols, x_full, y_local, LANES), jnp.float32),
+            pltpu.VMEM((devices, 2, y_local * SUBLANES, LANES), jnp.float32),
+            pltpu.VMEM((cols, 2, y_full * SUBLANES, LANES), jnp.float32),
+            pltpu.VMEM((2, y_full // LANES, z_full * SUBLANES, LANES), jnp.float32),
+            pltpu.SemaphoreType.DMA(((cols + 1) * (x_full // LANES) + 3,)),
+            pltpu.SemaphoreType.DMA((2 + y_full // LANES,)),
+            pltpu.SemaphoreType.DMA((devices,)),
+            pltpu.SemaphoreType.DMA((devices,)),
+            pltpu.SemaphoreType.DMA((devices,)),
+            pltpu.SemaphoreType.DMA((devices,)),
+        ],
+        compiler_params=pltpu.CompilerParams(
+            collective_id=0, has_side_effects=True, vmem_limit_bytes=56 * 1024 * 1024
+        ),
+        cost_estimate=pl.CostEstimate(flops=flops, bytes_accessed=16 * coefficients.size, transcendentals=0),
+    )(
+        coefficients.reshape(2, z_local * y_local, x_full),
+        real_bands.reshape(cols, z_local * y_local, x_full),
+        jnp.asarray(x_table),
+        jnp.asarray(z_table),
+        jnp.asarray(y_table),
+    )
+    return out.reshape(2, 1, z_full, SUBLANES, y_full), table[None]
+
+
 def local(coefficients, real_bands):
+    rows = lax.axis_size("row")
+    cols = lax.axis_size("col")
+    _, bands, z_local, y_local, x_full = coefficients.shape
+    fits = (
+        bands == 1
+        and real_bands.shape[0] == cols
+        and z_local == LANES
+        and y_local % (2 * SUBLANES) == 0
+        and x_full == SUBLANES * rows * cols
+        and x_full % (2 * LANES) == 0
+        and rows % 2 == 0
+    )
+    if fits:
+        return fused(coefficients, real_bands, rows, cols)
+    return general(coefficients, real_bands)
+
+
+def general(coefficients, real_bands):
     rows = lax.axis_size("row")
     cols = lax.axis_size("col")
     devices = rows * cols

time: 218 us -> 209 us (0.959)
  Pallas kernels: 0 us -> 201 us
  waiting for transfers between devices: 159 us -> 0 us
  local copies, waits for them, and re-layouts: 27.5 us -> 6.65 us
  matrix products: 18.3 us -> 0 us
  starting transfers between devices: 11.3 us -> 0 us
    pallas_call x0 -> x1, Pallas kernels: none -> 201 us  [fused(): pl.pallas_call(functools.partial(kernel, rows, cols, y_local), out_shape=...]
    all_to_all x2 -> x0, waiting for transfers between devices: 159 us -> none  [the longest x1 81.9 us: local(): moved = lax.all_to_all(first, axes, split_axis=0, concat_axis=0, tiled=True)]
    dot_general x3 -> x0, matrix products: 18.3 us -> none  [the longest x1 7.07 us: local(): jnp.einsum('cbzyk,ckedq->debyqz', coefficients, x_table, precision=precis...]
    transpose x3 -> x0, local copies, waits for them, and re-layouts: 14.3 us -> none  [the longest x1 6.57 us: local(): turned = jnp.transpose(turned, (4, 0, 1, 5, 3, 2))]
    all_to_all x2 -> x0, starting transfers between devices: 11.3 us -> none  [the longest x1 7.16 us: local(): moved = lax.all_to_all(first, axes, split_axis=0, concat_axis=0, tiled=True)]
    unnamed x7 -> x4, local copies, waits for them, and re-layouts: 13.2 us -> 6.65 us
  transfers between devices with their start and end apart: 2 -> 0, of which waited for: 2 -> 0; matrix products, arithmetic and copies ran while one was open for 13% -> 0% of each run, Pallas kernels for 0% -> 0%
where the time goes in v2:
time: 209 us; the launch traced here: 208 us
  Pallas kernels  201 us (96%)
  local copies, waits for them, and re-layouts  6.65 us (3%)
    pallas_call x1, Pallas kernels, fused(): pl.pallas_call(functools.partial(kernel, rows, cols, y_local), out_shape=...  201 us
    unnamed x4, local copies, waits for them, and re-layouts  6.65 us

profile of v2, /device:TPU:1, one launch (start us, length us, event | category | flops | bytes accessed | tf_op | source)
XLA Modules:
  0.0 208.4 jit_solution(6917244178755855227)
XLA Ops:
  0.6 201.1 %shard_map.68 = (f32[2,2048,256]{2,1,0:T(8,128)}, f32[16,256,256]{2,1,0:T(8,128)}) custom-call(f32[2,2048,256]{2,1,0:T(8,128)} %bitcast.8, f32[2,2048,256]{2,1,0:T(8,128)} %bitcast.9, bf16[2,512,512]{2,1,0:T(8,128)(2,1)} %constant.4.clone.x_table.z_table, bf16[2,512,512]{2,1,0:T(8,128)(2,1)} %constant.4.clone.x_table.z_table, ...), custom_call_target="tpu_custom_call" | custom-call | flops 19327352832 | bytes 16777216 | tf_op jit(solution)/shard_map/pallas_call | solution.py:267
  201.8 0.0 copy-start
  201.8 4.6 %copy.10 = f32[2,1,256,8,256]{4,3,2,1,0:T(8,128)} copy(f32[2,1,256,8,256]{4,3,2,1,0:T(8,128)} %bitcast.7) | data formatting | bytes 8388608
  206.4 0.0 copy-done
  206.4 2.0 copy.11
Async XLA Ops:
  201.8 4.7 %copy-start = (f32[16,256,256]{2,1,0:T(8,128)S(1)}, f32[16,256,256]{2,1,0:T(8,128)}, u32[]{:S(2)}) copy-start(f32[16,256,256]{2,1,0:T(8,128)} %get-tuple-element.5) | copy-start | bytes 12582916

commit v3 on v2

--- a/solution.py
+++ b/solution.py
@@ -73,30 +73,42 @@
     def number(by_col, by_half, step):
         return (by_col * 2 + by_half) * half_rows + step
 
-    groups = [(by_col, by_half) for by_half in (1, 0) for by_col in range(cols)]
-
-    def each_step(group, do):
-        own = group == (0, 0)
-
+    groups = [(by_col, by_half) for by_col in range(cols) for by_half in (1, 0)]
+
+    def each_step(chosen, do):
         def body(step, _):
-            do(*group, step)
+            for group in chosen:
+                if group == (0, 0):
+                    pl.when(step > 0)(functools.partial(do, *group, step))
+                else:
+                    do(*group, step)
             return 0
 
-        lax.fori_loop(1 if own else 0, half_rows, body, 0)
+        lax.fori_loop(0, half_rows, body, 0)
 
     barrier = pltpu.get_barrier_semaphore()
 
     def greet(by_col, by_half, step):
         pl.semaphore_signal(barrier, inc=1, device_id=target(by_col, by_half, step), device_id_type=MESH)
 
-    for group in groups:
-        each_step(group, greet)
+    each_step(groups, greet)
 
     def load(k, src, dst):
         return pltpu.make_async_copy(src, dst, load_sem.at[k])
 
-    def load_band(b, tile):
-        return load(b * x_tiles + tile, bands.at[b, :, pl.ds(tile * LANES, LANES)], band_in.at[b, tile])
+    half_tiles = x_tiles // 2
+
+    def lead(by_half):
+        return (half + by_half) % 2 * half_tiles
+
+    def load_bands(by_col, by_half):
+        b = (col + by_col) % cols
+        made = []
+        for at in range(half_tiles):
+            tile = lead(by_half) + at
+            lanes = pl.ds(pl.multiple_of(tile * LANES, LANES), LANES)
+            made.append(load((by_col * 2 + by_half) * half_tiles + at, bands.at[b, :, lanes], band_in.at[b, tile]))
+        return made
 
     k = cols * x_tiles
     loads = [
@@ -106,22 +118,24 @@
     ]
     for tile in range(x_tiles):
         loads.append(load(k + 3 + tile, coefficients.at[:, :, pl.ds(tile * LANES, LANES)], source.at[:, tile]))
-    for by_col in range(cols):
-        for tile in range(x_tiles):
-            load_band((col + by_col) % cols, tile).start()
+    for group in groups[:2]:
+        for one in load_bands(*group):
+            one.start()
     for one in loads:
         one.start()
+    for group in groups[2:]:
+        for one in load_bands(*group):
+            one.start()
 
     def turn(by_col, by_half):
         b = (col + by_col) % cols
-        half_tiles = x_tiles // 2
-        lead = (half + by_half) % 2 * half_tiles
+        first_tile = lead(by_half)
         flat = turned.reshape(cols, x_full * y_local, LANES)
 
         def body(y, _):
             for at in range(half_tiles):
-                plane = band_in[b, lead + at, pl.ds(y, LANES, stride=y_local), :]
-                flat[b, pl.ds((lead + at) * LANES * y_local + y, LANES, stride=y_local), :] = plane.T
+                plane = band_in[b, first_tile + at, pl.ds(y, LANES, stride=y_local), :]
+                flat[b, pl.ds((first_tile + at) * LANES * y_local + y, LANES, stride=y_local), :] = plane.T
             return 0
 
         lax.fori_loop(0, y_local, body, 0)
@@ -157,11 +171,15 @@
     def send_band(by_col, by_half, step):
         band_copy(by_col, by_half, step, row, col).start()
 
-    for tile in range(x_tiles):
-        load_band(col, tile).wait()
+    for one in load_bands(0, 1):
+        one.wait()
     turn(0, 1)
     pl.semaphore_wait(barrier, rows * cols - 1)
-    each_step((0, 1), send_band)
+    each_step([(0, 1)], send_band)
+    for one in load_bands(0, 0):
+        one.wait()
+    turn(0, 0)
+    each_step([(0, 0)], send_band)
 
     for one in loads:
         one.wait()
@@ -184,19 +202,7 @@
 
     lax.fori_loop(0, y_local // 2, x_step, 0)
 
-    def send_first(step, _):
-        for group in groups:
-            if group == (0, 0):
-
-                @pl.when(step > 0)
-                def _():
-                    first_copy(*group, step, row, col).start()
-
-            else:
-                first_copy(*group, step, row, col).start()
-        return 0
-
-    lax.fori_loop(0, half_rows, send_first, 0)
+    each_step(groups, lambda *at: first_copy(*at, row, col).start())
     own_first = pltpu.make_async_copy(
         first.at[row * cols + col],
         arrived.at[col, :, pl.ds(pl.multiple_of(row * block, SUBLANES), block)],
@@ -204,13 +210,11 @@
     )
     own_first.start()
 
-    for by_col in range(1, cols):
-        for tile in range(x_tiles):
-            load_band((col + by_col) % cols, tile).wait()
-    for group in groups:
-        if group != (0, 1):
-            turn(*group)
-            each_step(group, send_band)
+    for group in groups[2:]:
+        for one in load_bands(*group):
+            one.wait()
+        turn(*group)
+    each_step(groups[2:], send_band)
     own_band = pltpu.make_async_copy(
         turned.at[col, pl.ds(row * x_rows, x_rows)],
         table_out.at[
@@ -223,8 +227,7 @@
     own_band.start()
 
     own_first.wait()
-    for group in groups:
-        each_step(group, lambda *at: first_copy(*at, *origin(*at)).wait_recv())
+    each_step(groups, lambda *at: first_copy(*at, *origin(*at)).wait_recv())
 
     def final_step(x, _):
         pieces = [
@@ -250,10 +253,9 @@
     for store in stores:
         store.wait()
     own_band.wait()
-    for group in groups:
-        each_step(group, lambda *at: first_copy(*at, *origin(*at)).wait_send())
-        each_step(group, lambda *at: band_copy(*at, *origin(*at)).wait_send())
-        each_step(group, lambda *at: band_copy(*at, *origin(*at)).wait_recv())
+    each_step(groups, lambda *at: first_copy(*at, *origin(*at)).wait_send())
+    each_step(groups, lambda *at: band_copy(*at, *origin(*at)).wait_send())
+    each_step(groups, lambda *at: band_copy(*at, *origin(*at)).wait_recv())
 
 
 def fused(coefficients, real_bands, rows, cols):

time: 209 us -> 199 us (0.952)
  Pallas kernels: 201 us -> 192 us
    pallas_call x1, Pallas kernels: 201 us -> 192 us  [fused(): pl.pallas_call(functools.partial(kernel, rows, cols, y_local), out_shape=...]
where the time goes in v3:
time: 199 us
  Pallas kernels  192 us (96%)
  local copies, waits for them, and re-layouts  6.65 us (3%)
    pallas_call x1, Pallas kernels, fused(): pl.pallas_call(functools.partial(kernel, rows, cols, y_local), out_shape=...  192 us
    unnamed x4, local copies, waits for them, and re-layouts  6.65 us

profile of v3, /device:TPU:1, one launch (start us, length us, event | category | flops | bytes accessed | tf_op | source)
XLA Modules:
  0.0 199.0 jit_solution(7066699723546102150)
XLA Ops:
  0.6 191.7 %shard_map.68 = (f32[2,2048,256]{2,1,0:T(8,128)}, f32[16,256,256]{2,1,0:T(8,128)}) custom-call(f32[2,2048,256]{2,1,0:T(8,128)} %bitcast.8, f32[2,2048,256]{2,1,0:T(8,128)} %bitcast.9, bf16[2,512,512]{2,1,0:T(8,128)(2,1)} %constant.4.clone.x_table.z_table, bf16[2,512,512]{2,1,0:T(8,128)(2,1)} %constant.4.clone.x_table.z_table, ...), custom_call_target="tpu_custom_call" | custom-call | flops 19327352832 | bytes 16777216 | tf_op jit(solution)/shard_map/pallas_call | solution.py:269
  192.3 0.0 copy-start
  192.4 4.6 %copy.10 = f32[2,1,256,8,256]{4,3,2,1,0:T(8,128)} copy(f32[2,1,256,8,256]{4,3,2,1,0:T(8,128)} %bitcast.7) | data formatting | bytes 8388608
  197.0 0.0 copy-done
  197.0 2.0 %copy.11 = f32[1,16,256,256]{3,2,1,0:T(8,128)} copy(f32[1,16,256,256]{3,2,1,0:T(8,128)S(1)} %bitcast.6) | data formatting | bytes 8388608
Async XLA Ops:
  192.3 4.7 %copy-start = (f32[16,256,256]{2,1,0:T(8,128)S(1)}, f32[16,256,256]{2,1,0:T(8,128)}, u32[]{:S(2)}) copy-start(f32[16,256,256]{2,1,0:T(8,128)} %get-tuple-element.5) | copy-start | bytes 12582916

commit v4 on v3

--- a/solution.py
+++ b/solution.py
@@ -214,7 +214,22 @@
         for one in load_bands(*group):
             one.wait()
         turn(*group)
-    each_step(groups[2:], send_band)
+
+    def send_rest(step, _):
+        for group in groups:
+
+            def sent(group=group):
+                first_copy(*group, step, *origin(*group, step)).wait_send()
+
+            if group == (0, 0):
+                pl.when(step > 0)(sent)
+            else:
+                sent()
+        for group in groups[2:]:
+            send_band(*group, step)
+        return 0
+
+    lax.fori_loop(0, half_rows, send_rest, 0)
     own_band = pltpu.make_async_copy(
         turned.at[col, pl.ds(row * x_rows, x_rows)],
         table_out.at[
@@ -253,7 +268,6 @@
     for store in stores:
         store.wait()
     own_band.wait()
-    each_step(groups, lambda *at: first_copy(*at, *origin(*at)).wait_send())
     each_step(groups, lambda *at: band_copy(*at, *origin(*at)).wait_send())
     each_step(groups, lambda *at: band_copy(*at, *origin(*at)).wait_recv())
 
@@ -269,11 +283,11 @@
     out, table = pl.pallas_call(
         functools.partial(kernel, rows, cols, y_local),
         out_shape=[
-            jax.ShapeDtypeStruct((2, z_full * SUBLANES, y_full), jnp.float32),
-            jax.ShapeDtypeStruct((x_rows, y_full, z_full), jnp.float32),
+            pltpu.VMEM((2, z_full * SUBLANES, y_full), jnp.float32),
+            pltpu.VMEM((x_rows, y_full, z_full), jnp.float32),
         ],
         in_specs=[pl.BlockSpec(memory_space=pl.ANY)] * 5,
-        out_specs=[pl.BlockSpec(memory_space=pl.ANY)] * 2,
+        out_specs=[pl.BlockSpec(memory_space=pltpu.VMEM)] * 2,
         scratch_shapes=[
             pltpu.VMEM((2, x_full // LANES, z_local * y_local, LANES), jnp.float32),
             pltpu.VMEM((cols, x_full // LANES, z_local * y_local, LANES), jnp.float32),
@@ -292,7 +306,7 @@
             pltpu.SemaphoreType.DMA((devices,)),
         ],
         compiler_params=pltpu.CompilerParams(
-            collective_id=0, has_side_effects=True, vmem_limit_bytes=56 * 1024 * 1024
+            collective_id=0, has_side_effects=True, vmem_limit_bytes=40 * 1024 * 1024
         ),
         cost_estimate=pl.CostEstimate(flops=flops, bytes_accessed=16 * coefficients.size, transcendentals=0),
     )(

time: 199 us -> 199 us (level)
    unnamed x4 -> x6, local copies, waits for them, and re-layouts: 6.65 us -> 6.47 us
where the time goes in v4:
time: 199 us
  Pallas kernels  192 us (96%)
  local copies, waits for them, and re-layouts  6.47 us (3%)
    pallas_call x1, Pallas kernels, fused(): pl.pallas_call(functools.partial(kernel, rows, cols, y_local), out_shape=...  192 us
    unnamed x6, local copies, waits for them, and re-layouts  6.47 us

profile of v4, /device:TPU:1, one launch (start us, length us, event | category | flops | bytes accessed | tf_op | source)
XLA Modules:
  0.0 199.1 jit_solution(1370517343591383648)
XLA Ops:
  0.6 0.0 copy-start
  0.6 1.2 copy-done
  1.9 0.0 copy-start.1
  1.9 1.2 copy-done.1
  3.1 192.0 %shard_map.68 = (f32[2,2048,256]{2,1,0:T(8,128)S(1)}, f32[16,256,256]{2,1,0:T(8,128)S(1)}) custom-call(f32[2,2048,256]{2,1,0:T(8,128)} %bitcast.8, f32[2,2048,256]{2,1,0:T(8,128)} %bitcast.9, bf16[2,512,512]{2,1,0:T(8,128)(2,1)S(1)} %copy-done.1, bf16[2,512,512]{2,1,0:T(8,128)(2,1)S(1)} %copy-done.1, bf16[2,512,512]{2,1,0:T(8,128)(2,1)S(1)} %copy-done), custom_call_target="tpu_custom_call" | custom-call | flops 19327352832 | bytes 16777216 | tf_op jit(solution)/shard_map/pallas_call | solution.py:283
  195.1 2.0 %copy.10 = f32[2,1,256,8,256]{4,3,2,1,0:T(8,128)} copy(f32[2,1,256,8,256]{4,3,2,1,0:T(8,128)S(1)} %bitcast.7) | data formatting | bytes 8388608
  197.1 2.0 %copy.11 = f32[1,16,256,256]{3,2,1,0:T(8,128)} copy(f32[1,16,256,256]{3,2,1,0:T(8,128)S(1)} %bitcast.6) | data formatting | bytes 8388608
Async XLA Ops:
  0.6 1.2 copy-start
  1.9 1.2 copy-start.1

commit v5 on v3

--- a/solution.py
+++ b/solution.py
@@ -86,6 +86,20 @@
 
         lax.fori_loop(0, half_rows, body, 0)
 
+    phase = place % 2
+
+    def each_turn(chosen, do):
+        def body(step, _):
+            for by_col, by_half in chosen:
+                by_half = (by_half + phase) % 2
+                if by_col == 0:
+                    pl.when(by_half + step > 0)(functools.partial(do, by_col, by_half, step))
+                else:
+                    do(by_col, by_half, step)
+            return 0
+
+        lax.fori_loop(0, half_rows, body, 0)
+
     barrier = pltpu.get_barrier_semaphore()
 
     def greet(by_col, by_half, step):
@@ -118,8 +132,8 @@
     ]
     for tile in range(x_tiles):
         loads.append(load(k + 3 + tile, coefficients.at[:, :, pl.ds(tile * LANES, LANES)], source.at[:, tile]))
-    for group in groups[:2]:
-        for one in load_bands(*group):
+    for by_col, by_half in groups[:2]:
+        for one in load_bands(by_col, (by_half + phase) % 2):
             one.start()
     for one in loads:
         one.start()
@@ -171,15 +185,13 @@
     def send_band(by_col, by_half, step):
         band_copy(by_col, by_half, step, row, col).start()
 
-    for one in load_bands(0, 1):
-        one.wait()
-    turn(0, 1)
-    pl.semaphore_wait(barrier, rows * cols - 1)
-    each_step([(0, 1)], send_band)
-    for one in load_bands(0, 0):
-        one.wait()
-    turn(0, 0)
-    each_step([(0, 0)], send_band)
+    for by_half in (1, 0):
+        for one in load_bands(0, (by_half + phase) % 2):
+            one.wait()
+        turn(0, (by_half + phase) % 2)
+        if by_half == 1:
+            pl.semaphore_wait(barrier, rows * cols - 1)
+        each_turn([(0, by_half)], send_band)
 
     for one in loads:
         one.wait()
@@ -202,7 +214,7 @@
 
     lax.fori_loop(0, y_local // 2, x_step, 0)
 
-    each_step(groups, lambda *at: first_copy(*at, row, col).start())
+    each_turn(groups, lambda *at: first_copy(*at, row, col).start())
     own_first = pltpu.make_async_copy(
         first.at[row * cols + col],
         arrived.at[col, :, pl.ds(pl.multiple_of(row * block, SUBLANES), block)],
@@ -214,7 +226,8 @@
         for one in load_bands(*group):
             one.wait()
         turn(*group)
-    each_step(groups[2:], send_band)
+
+    each_turn(groups[2:], send_band)
     own_band = pltpu.make_async_copy(
         turned.at[col, pl.ds(row * x_rows, x_rows)],
         table_out.at[
@@ -269,11 +282,11 @@
     out, table = pl.pallas_call(
         functools.partial(kernel, rows, cols, y_local),
         out_shape=[
-            jax.ShapeDtypeStruct((2, z_full * SUBLANES, y_full), jnp.float32),
-            jax.ShapeDtypeStruct((x_rows, y_full, z_full), jnp.float32),
+            pltpu.VMEM((2, z_full * SUBLANES, y_full), jnp.float32),
+            pltpu.VMEM((x_rows, y_full, z_full), jnp.float32),
         ],
         in_specs=[pl.BlockSpec(memory_space=pl.ANY)] * 5,
-        out_specs=[pl.BlockSpec(memory_space=pl.ANY)] * 2,
+        out_specs=[pl.BlockSpec(memory_space=pltpu.VMEM)] * 2,
         scratch_shapes=[
             pltpu.VMEM((2, x_full // LANES, z_local * y_local, LANES), jnp.float32),
             pltpu.VMEM((cols, x_full // LANES, z_local * y_local, LANES), jnp.float32),
@@ -292,7 +305,7 @@
             pltpu.SemaphoreType.DMA((devices,)),
         ],
         compiler_params=pltpu.CompilerParams(
-            collective_id=0, has_side_effects=True, vmem_limit_bytes=56 * 1024 * 1024
+            collective_id=0, has_side_effects=True, vmem_limit_bytes=55 * 1024 * 1024
         ),
         cost_estimate=pl.CostEstimate(flops=flops, bytes_accessed=16 * coefficients.size, transcendentals=0),
     )(

time: 199 us -> 199 us (level)
  local copies, waits for them, and re-layouts: 6.65 us -> 4.03 us
    unnamed x4 -> x2, local copies, waits for them, and re-layouts: 6.65 us -> 4.03 us
where the time goes in v5:
time: 199 us; the launch traced here: 198 us
  Pallas kernels  193 us (97%)
  local copies, waits for them, and re-layouts  4.03 us (2%)
    pallas_call x1, Pallas kernels, fused(): pl.pallas_call(functools.partial(kernel, rows, cols, y_local), out_shape=...  193 us
    unnamed x2, local copies, waits for them, and re-layouts  4.03 us

profile of v5, /device:TPU:1, one launch (start us, length us, event | category | flops | bytes accessed | tf_op | source)
XLA Modules:
  0.0 197.6 jit_solution(1373990030961230381)
XLA Ops:
  0.6 192.9 %shard_map.68 = (f32[2,2048,256]{2,1,0:T(8,128)S(1)}, f32[16,256,256]{2,1,0:T(8,128)S(1)}) custom-call(f32[2,2048,256]{2,1,0:T(8,128)} %bitcast.8, f32[2,2048,256]{2,1,0:T(8,128)} %bitcast.9, bf16[2,512,512]{2,1,0:T(8,128)(2,1)} %constant.4.clone.x_table.z_table, bf16[2,512,512]{2,1,0:T(8,128)(2,1)} %constant.4.clone.x_table.z_table, ...), custom_call_target="tpu_custom_call" | custom-call | flops 19327352832 | bytes 16777216 | tf_op jit(solution)/shard_map/pallas_call | solution.py:282
  193.6 2.0 %copy.10 = f32[2,1,256,8,256]{4,3,2,1,0:T(8,128)} copy(f32[2,1,256,8,256]{4,3,2,1,0:T(8,128)S(1)} %bitcast.7) | data formatting | bytes 8388608
  195.6 2.0 %copy.11 = f32[1,16,256,256]{3,2,1,0:T(8,128)} copy(f32[1,16,256,256]{3,2,1,0:T(8,128)S(1)} %bitcast.6) | data formatting | bytes 8388608
